TPU v7x, 128 devices: a whole 4x4x4 slice. The times are simulated.
128 devices in a mesh: img: 16 (over z, y), tile: 8 (over x, core).
Axes of the slice: x: 4, y: 4, z: 4, core: 2. Of those that a mesh axis runs over, the one named last changes fastest.
Arguments:
- spins: float32 [16, 3, 16, 256, 256], P('img', None, None, 'tile'), may hold values from -4.5 to 4.5
- aniso: float32 [16, 256, 256], P(None, 'tile'), may hold values from 0.2 to 2
Outputs:
- path: float32 [16, 3, 16, 256, 256], P('img', None, None, 'tile')
All inputs are finite; a program needn't handle non-finite values.
Results may differ from a plain program's by a relative error of at most 0.0003.
Values sent between devices are 32-bit elements; how exact they have to be, the bound alone decides.
No kernel may reach another device: no remote copies, remote signals or barrier semaphores. Data moves between devices by JAX's collectives and lax.ppermute only.
A program may use at most 128 MiB of HBM per device.

v0:
```python
import jax
import jax.numpy as jnp
from jax import lax
from jax.sharding import Mesh
from jax.sharding import PartitionSpec as P

OUTER = 2
INNER = 3
IMG = ("img_0", "img_1")
TILE = ("tile_0", "tile_1")
IMG_TILE = ("img_0", "img_1", "tile_0", "tile_1")
exchange_coef = 1.0
cubic_coef = 0.5
spring_coef = 20.0
step_scale = 0.25
epsilon = 1e-06


def padded_2(cells, sides, width):
    for axis, dim in sides:
        count = lax.axis_size(axis)
        ends = count - 1
        head = lax.slice_in_dim(cells, 0, width, axis=dim)
        tail = lax.slice_in_dim(cells, cells.shape[dim] - width, cells.shape[dim], axis=dim)
        cells = jnp.concatenate(
            [
                lax.ppermute(tail, axis, [(i, (i + 1) % count) for i in range(ends)]),
                cells,
                lax.ppermute(head, axis, [((i + 1) % count, i) for i in range(ends)]),
            ],
            axis=dim,
        )
    return cells


def from_everyone(shard, axis):
    peers = lax.axis_size(axis)
    return lax.all_to_all(
        jnp.broadcast_to(shard[None], (peers, *shard.shape)), axis, 0, 0, tiled=True
    )


def folded_in_pairs(pieces, combine):
    while len(jax.tree.leaves(pieces)[0]) > 1:
        pieces = jax.vmap(combine)(*(pieces[side::2] for side in (0, 1)))
    return pieces[0]


def carried_in(shard, axis, combine, identity):
    peers, here = (lax.axis_size(axis), lax.axis_index(axis))
    passed = jnp.arange(peers) < here

    def kept(part, zero, own):
        part = jnp.where(
            passed.reshape(-1, *(1 for _ in own.shape)), part, jnp.asarray(zero, own.dtype)
        )
        return part

    pieces = from_everyone(shard, axis)
    return folded_in_pairs(kept(pieces, identity, shard), combine)


def over_copies(shard, axis):
    return from_everyone(shard, axis).sum(axis=0)


def over_axes(shard, axes):
    for axis in axes:
        shard = lax.psum(shard, axis)
    return shard


def laplace(field):
    widths = [(0, 0)] * (field.ndim - 4) + [(0, 0), (1, 1), (0, 0), (1, 1)]
    padded = jnp.pad(field, widths)
    centre = padded[..., 1:-1, 1:-1, 1:-1]
    beside_all = padded[..., 2:, 1:-1, 1:-1] + padded[..., :-2, 1:-1, 1:-1]
    beside_all = beside_all + padded[..., 1:-1, 2:, 1:-1] + padded[..., 1:-1, :-2, 1:-1]
    beside_all = beside_all + padded[..., 1:-1, 1:-1, 2:] + padded[..., 1:-1, 1:-1, :-2]
    return beside_all - 6.0 * centre


def axis_select():
    return (jnp.arange(3) == 2).astype(jnp.float32)[:, None, None, None]


def force_field(middle_ext, coefs):
    middle = middle_ext[..., 1:-1, :]
    square_norm = jnp.sum(middle * middle, axis=-4, keepdims=True)
    return (
        exchange_coef * laplace(middle_ext)
        + coefs * middle * axis_select()
        - cubic_coef * (square_norm - 1.0) * middle
    )


def hessian_point(middle, vector, coefs):
    square_norm = jnp.sum(middle * middle, axis=-4, keepdims=True)
    projected = jnp.sum(middle * vector, axis=-4, keepdims=True)
    return coefs * vector * axis_select() - cubic_coef * (
        (square_norm - 1.0) * vector + 2.0 * middle * projected
    )


def add_pair(earlier, later):
    return earlier + later


def body(spins, aniso):
    local_images = spins.shape[0]
    width_x = spins.shape[3]
    img_count = lax.axis_size(IMG)
    tile_count = lax.axis_size(TILE)
    images = local_images * img_count
    cell_count = float(
        images * spins.shape[1] * spins.shape[2] * width_x * tile_count * spins.shape[4]
    )
    first_image = lax.axis_index(IMG) * local_images
    image_index = first_image + jnp.arange(local_images, dtype=jnp.int32)
    segment_live = (image_index < images - 1).astype(jnp.float32)
    interior = ((image_index > 0) & (image_index < images - 1)).astype(jnp.float32)
    target = image_index.astype(jnp.float32) / (images - 1)
    rim_depth = 1
    cycle_mask = 1.0
    current = spins
    for outer_step in range(OUTER):
        repeated = current
        framed_all = padded_2(repeated, ((IMG, 0), (TILE, 3)), rim_depth)
        before_img = framed_all[:-2]
        own_framed = framed_all[1:-1]
        after_img = framed_all[2:]
        difference = (after_img - own_framed)[..., rim_depth : rim_depth + width_x, :]
        middle_seg = 0.5 * (own_framed + after_img)
        drive_own = force_field(middle_seg, aniso)
        diff_sq = jnp.sum(difference * difference, axis=(1, 2, 3, 4))
        drive_sq = jnp.sum(drive_own * drive_own, axis=(1, 2, 3, 4))
        diff_sq, drive_sq = lax.psum((diff_sq, drive_sq), TILE)
        seg_len = segment_live * jnp.sqrt(diff_sq + epsilon)
        drive_len = segment_live * jnp.sqrt(drive_sq + epsilon)
        offset = carried_in(jnp.sum(seg_len), IMG, add_pair, jnp.float32(0.0))
        path_len, drive_total = (
            over_copies(jnp.sum(seg_len), IMG),
            over_copies(jnp.sum(drive_len), IMG),
        )
        before_arc = offset + jnp.cumsum(seg_len) - seg_len
        time_step = path_len / drive_total
        spring_pull = (
            spring_coef * (before_arc / path_len - target) * (images - 1) / (2.0 * path_len)
        )
        spring_pull = spring_pull[:, None, None, None, None]
        interior_mask = interior[:, None, None, None, None]
        before_core = before_img[..., 1:-1, :]
        after_core = after_img[..., 1:-1, :]
        before_own = before_img[..., rim_depth : rim_depth + width_x, :]
        after_own = after_img[..., rim_depth : rim_depth + width_x, :]
        for inner_step in range(INNER):
            if inner_step == 0:
                own_ext = own_framed
            else:
                own_ext = padded_2(current, ((TILE, 3),), rim_depth)
            own_core = own_ext[..., 1:-1, :]
            middle_a = 0.5 * (before_img + own_ext)
            middle_b = 0.5 * (own_ext + after_img)
            res_a = (
                (own_core - before_core) / time_step - force_field(middle_a, aniso)
            ) * cycle_mask
            res_b = (
                (after_core - own_core) / time_step - force_field(middle_b, aniso)
            ) * cycle_mask
            res_sum = res_a + res_b
            adjoint_lap = laplace(padded_2(res_sum, ((TILE, 3),), 1))
            middle_a_own = middle_a[..., rim_depth : rim_depth + width_x, :]
            middle_b_own = middle_b[..., rim_depth : rim_depth + width_x, :]
            adjoint = exchange_coef * adjoint_lap
            adjoint = (
                adjoint
                + hessian_point(middle_a_own, res_a, aniso)
                + hessian_point(middle_b_own, res_b, aniso)
            )
            gradients = (
                res_a - res_b - 0.5 * time_step * adjoint + spring_pull * (after_own - before_own)
            )
            gradients = gradients * interior_mask
            grad_total = over_axes(jnp.sum(gradients * gradients), IMG_TILE)
            grad_scale = jnp.sqrt(grad_total / cell_count + epsilon)
            current = current - step_scale * gradients / grad_scale
    return current


def solution(mesh):
    split = Mesh(mesh.devices.reshape(4, 4, 4, 2), ("img_0", "img_1", "tile_0", "tile_1"))
    return jax.shard_map(
        body,
        mesh=split,
        in_specs=(P(IMG, None, None, TILE, None), P(None, TILE, None)),
        out_specs=P(IMG, None, None, TILE, None),
        check_vma=False,
    )
```

profile of v0, /device:TPU:1, one launch (start us, length us, event | category | flops | bytes accessed | tf_op | source)
XLA Modules:
  0.0 635.0 jit_solution(12374536469458918659)
XLA Ops:
  7.9 31.6 %collective-permute-done = f32[1,3,16,32,256]{4,2,3,1,0:T(8,128)S(1)} collective-permute-done((f32[1,3,16,32,256]{4,2,3,1,0:T(8,128)S(1)}, f32[1,3,16,32,256]{4,2,3,1,0:T(8,128)S(1)}, u32[]{:S(2)}, u32[]{:S(2)}) %collective-permute-start) | collective-permute-done | bytes 1572896 | tf_op jit(solution)/shard_map/ppermute | solution.py:27
  69.8 11.1 %all-reduce.19 = (f32[1]{0:T(128)}, f32[1]{0:T(128)}) all-reduce(f32[1]{0:T(128)} %bitcast.1, f32[1]{0:T(128)} %bitcast.3), channel_id=1, replica_groups=mesh['img_0'=4,'img_1'=4,'tile_0'=4,'tile_1'=2] {'tile_0','tile_1'}, use_global_device_ids=true, to_apply=%region_1.2 | all-reduce | flops 2 | bytes 16 | tf_op jit(solution)/shard_map/psum | solution.py:137
  82.7 9.1 %all-to-all-start = ((f32[16,1,1]{2,1,0:T(1,128)}), f32[16,1,1]{2,1,0:T(1,128)S(1)}, u32[]{:S(2)}, u32[]{:S(2)}) async-start(f32[16,1,1]{2,1,0:T(1,128)} %broadcast_in_dim.22), calls=%async_computation | async-start | bytes 16384 | tf_op jit(solution)/shard_map/all_to_all | solution.py:38
  110.4 8.4 %multiply_reduce_fusion.28 = (f32[16,32,256]{2,0,1:T(8,128)S(1)}, f32[1,3,16,32,256]{4,2,3,1,0:T(8,128)S(1)}, f32[16,32,256]{2,0,1:T(8,128)S(1)}, f32[1,3,16,32,256]{4,2,3,1,0:T(8,128)S(1)}) fusion(f32[1,3,16,34,256]{4,2,3,1,0:T(8,128)} %copy-done.2, f32[16,32,256]{2,0,1:T(8,128)S(1)} %get-tuple-element.128, f32[3]{0:T(128)S(1)} %compare_convert_fusion, ...), kind=kLoop, calls=%fused_computation.318 | loop fusion | flops 8388608 | bytes 19496976 | tf_op jit(solution)/shard_map/reduce_sum | solution.py:99
  138.6 7.4 %multiply_reduce_fusion.26 = (f32[]{:T(128)}, f32[1,3,16,32,256]{4,2,3,1,0:T(8,128)}, f32[1,3,16,32,256]{4,2,3,1,0:T(8,128)}) fusion(f32[]{:T(128)} %bitcast.10, f32[16,32,256]{2,0,1:T(8,128)} %broadcast_multiply_fusion.10, f32[1,3,16,34,256]{4,2,3,1,0:T(8,128)S(1)} %get-tuple-element.68, f32[1,3,16,32,256]{4,2,3,1,0:T(8,128)} %copy-done.41, ...), kind=kLoop, calls=%fused_computation.315 | loop fusion | flops 13369343 | bytes 23167004 | tf_op jit(solution)/shard_map/reduce_sum | solution.py:184
  145.9 7.5 %psum.198 = f32[]{:T(128)} all-reduce(f32[]{:T(128)} %get-tuple-element.46), channel_id=1, replica_groups=mesh['img_0'=4,'img_1'=4,'tile_0'=4,'tile_1'=2] {'img_0'}, use_global_device_ids=true, to_apply=%region_11.12 | all-reduce | flops 1 | bytes 8 | tf_op jit(solution)/shard_map/psum | solution.py:69
  153.4 7.7 %psum.199 = f32[]{:T(128)} all-reduce(f32[]{:T(128)} %psum.198), channel_id=1, replica_groups=mesh['img_0'=4,'img_1'=4,'tile_0'=4,'tile_1'=2] {'img_1'}, use_global_device_ids=true, to_apply=%region_12.13 | all-reduce | flops 1 | bytes 8 | tf_op jit(solution)/shard_map/psum | solution.py:69
  161.0 7.3 %psum.200 = f32[]{:T(128)} all-reduce(f32[]{:T(128)} %psum.199), channel_id=1, replica_groups=mesh['img_0'=4,'img_1'=4,'tile_0'=4,'tile_1'=2] {'tile_0'}, use_global_device_ids=true, to_apply=%region_13.14 | all-reduce | flops 1 | bytes 8 | tf_op jit(solution)/shard_map/psum | solution.py:69
  168.3 10.6 %psum.201 = f32[]{:T(128)} all-reduce(f32[]{:T(128)} %psum.200), channel_id=1, replica_groups=mesh['img_0'=4,'img_1'=4,'tile_0'=4,'tile_1'=2] {'tile_1'}, use_global_device_ids=true, to_apply=%region_14.15 | all-reduce | flops 1 | bytes 8 | tf_op jit(solution)/shard_map/psum | solution.py:69
  194.6 7.8 %multiply_reduce_fusion.23 = (f32[16,32,256]{2,0,1:T(8,128)}, f32[1,3,16,32,256]{4,2,3,1,0:T(8,128)}, f32[16,32,256]{2,0,1:T(8,128)}, f32[1,3,16,32,256]{4,2,3,1,0:T(8,128)}) fusion(f32[1,3,16,34,256]{4,2,3,1,0:T(8,128)S(1)} %get-tuple-element.61, f32[16,32,256]{2,0,1:T(8,128)} %get-tuple-element.124, f32[3]{0:T(128)S(1)} %compare_convert_fusion, ...), kind=kLoop, calls=%fused_computation.311 | loop fusion | flops 13107200 | bytes 23265796 | tf_op jit(solution)/shard_map/reduce_sum | solution.py:99
  227.6 7.3 %psum.203 = f32[]{:T(128)} all-reduce(f32[]{:T(128)} %psum.202), channel_id=1, replica_groups=mesh['img_0'=4,'img_1'=4,'tile_0'=4,'tile_1'=2] {'img_1'}, use_global_device_ids=true, to_apply=%region_21.22 | all-reduce | flops 1 | bytes 8 | tf_op jit(solution)/shard_map/psum | solution.py:69
  235.0 7.1 %psum.204 = f32[]{:T(128)} all-reduce(f32[]{:T(128)} %psum.203), channel_id=1, replica_groups=mesh['img_0'=4,'img_1'=4,'tile_0'=4,'tile_1'=2] {'tile_0'}, use_global_device_ids=true, to_apply=%region_22.23 | all-reduce | flops 1 | bytes 8 | tf_op jit(solution)/shard_map/psum | solution.py:69
  242.1 8.7 %psum.205 = f32[]{:T(128)} all-reduce(f32[]{:T(128)} %psum.204), channel_id=1, replica_groups=mesh['img_0'=4,'img_1'=4,'tile_0'=4,'tile_1'=2] {'tile_1'}, use_global_device_ids=true, to_apply=%region_23.24 | all-reduce | flops 1 | bytes 8 | tf_op jit(solution)/shard_map/psum | solution.py:69
  265.9 7.7 %multiply_reduce_fusion.18 = (f32[16,32,256]{2,0,1:T(8,128)}, f32[1,3,16,32,256]{4,2,3,1,0:T(8,128)}, f32[16,32,256]{2,0,1:T(8,128)}, f32[1,3,16,32,256]{4,2,3,1,0:T(8,128)}) fusion(f32[1,3,16,34,256]{4,2,3,1,0:T(8,128)S(1)} %get-tuple-element.59, f32[16,32,256]{2,0,1:T(8,128)} %get-tuple-element.120, f32[3]{0:T(128)S(1)} %compare_convert_fusion, ...), kind=kLoop, calls=%fused_computation.305 | loop fusion | flops 13107200 | bytes 23265796 | tf_op jit(solution)/shard_map/reduce_sum | solution.py:99
  291.8 7.3 %psum.206 = f32[]{:T(128)} all-reduce(f32[]{:T(128)} %get-tuple-element.34), channel_id=1, replica_groups=mesh['img_0'=4,'img_1'=4,'tile_0'=4,'tile_1'=2] {'img_0'}, use_global_device_ids=true, to_apply=%region_29.30 | all-reduce | flops 1 | bytes 8 | tf_op jit(solution)/shard_map/psum | solution.py:69
  299.1 7.7 %psum.207 = f32[]{:T(128)} all-reduce(f32[]{:T(128)} %psum.206), channel_id=1, replica_groups=mesh['img_0'=4,'img_1'=4,'tile_0'=4,'tile_1'=2] {'img_1'}, use_global_device_ids=true, to_apply=%region_30.31 | all-reduce | flops 1 | bytes 8 | tf_op jit(solution)/shard_map/psum | solution.py:69
  313.8 8.5 %psum.209 = f32[]{:T(128)} all-reduce(f32[]{:T(128)} %psum.208), channel_id=1, replica_groups=mesh['img_0'=4,'img_1'=4,'tile_0'=4,'tile_1'=2] {'tile_1'}, use_global_device_ids=true, to_apply=%region_32.33 | all-reduce | flops 1 | bytes 8 | tf_op jit(solution)/shard_map/psum | solution.py:69
  330.2 32.1 %collective-permute-done.15 = f32[1,3,16,32,256]{4,2,3,1,0:T(8,128)S(1)} collective-permute-done((f32[1,3,16,32,256]{4,2,3,1,0:T(8,128)S(1)}, f32[1,3,16,32,256]{4,2,3,1,0:T(8,128)S(1)}, u32[]{:S(2)}, u32[]{:S(2)}) %collective-permute-start.15) | collective-permute-done | bytes 1572896 | tf_op jit(solution)/shard_map/ppermute | solution.py:29
  382.0 10.6 %all-reduce.18 = (f32[1]{0:T(128)}, f32[1]{0:T(128)}) all-reduce(f32[1]{0:T(128)} %bitcast.11, f32[1]{0:T(128)} %bitcast.13), channel_id=1, replica_groups=mesh['img_0'=4,'img_1'=4,'tile_0'=4,'tile_1'=2] {'tile_0','tile_1'}, use_global_device_ids=true, to_apply=%region_34.35 | all-reduce | flops 2 | bytes 16 | tf_op jit(solution)/shard_map/psum | solution.py:137
  420.3 8.1 %multiply_reduce_fusion.12 = (f32[16,32,256]{2,0,1:T(8,128)S(1)}, f32[1,3,16,32,256]{4,2,3,1,0:T(8,128)S(1)}, f32[16,32,256]{2,0,1:T(8,128)S(1)}, f32[1,3,16,32,256]{4,2,3,1,0:T(8,128)S(1)}) fusion(f32[1,3,16,34,256]{4,2,3,1,0:T(8,128)} %copy-done, f32[16,32,256]{2,0,1:T(8,128)S(1)} %get-tuple-element.116, f32[3]{0:T(128)S(1)} %compare_convert_fusion, ...), kind=kLoop, calls=%fused_computation.297 | loop fusion | flops 8388608 | bytes 19496976 | tf_op jit(solution)/shard_map/reduce_sum | solution.py:99
  448.5 7.3 %multiply_reduce_fusion.10 = (f32[]{:T(128)}, f32[1,3,16,32,256]{4,2,3,1,0:T(8,128)}, f32[1,3,16,32,256]{4,2,3,1,0:T(8,128)}) fusion(f32[]{:T(128)} %bitcast.10, f32[16,32,256]{2,0,1:T(8,128)} %broadcast_multiply_fusion.4, f32[1,3,16,34,256]{4,2,3,1,0:T(8,128)S(1)} %get-tuple-element.64, f32[1,3,16,32,256]{4,2,3,1,0:T(8,128)} %copy-done.39, ...), kind=kLoop, calls=%fused_computation.294 | loop fusion | flops 13369343 | bytes 23167004 | tf_op jit(solution)/shard_map/reduce_sum | solution.py:184
  455.7 7.8 %psum.212 = f32[]{:T(128)} all-reduce(f32[]{:T(128)} %get-tuple-element.25), channel_id=1, replica_groups=mesh['img_0'=4,'img_1'=4,'tile_0'=4,'tile_1'=2] {'img_0'}, use_global_device_ids=true, to_apply=%region_44.45 | all-reduce | flops 1 | bytes 8 | tf_op jit(solution)/shard_map/psum | solution.py:69
  463.5 7.6 %psum.213 = f32[]{:T(128)} all-reduce(f32[]{:T(128)} %psum.212), channel_id=1, replica_groups=mesh['img_0'=4,'img_1'=4,'tile_0'=4,'tile_1'=2] {'img_1'}, use_global_device_ids=true, to_apply=%region_45.46 | all-reduce | flops 1 | bytes 8 | tf_op jit(solution)/shard_map/psum | solution.py:69
  477.8 9.8 %psum.215 = f32[]{:T(128)} all-reduce(f32[]{:T(128)} %psum.214), channel_id=1, replica_groups=mesh['img_0'=4,'img_1'=4,'tile_0'=4,'tile_1'=2] {'tile_1'}, use_global_device_ids=true, to_apply=%region_47.48 | all-reduce | flops 1 | bytes 8 | tf_op jit(solution)/shard_map/psum | solution.py:69
  502.8 7.7 %multiply_reduce_fusion.7 = (f32[16,32,256]{2,0,1:T(8,128)}, f32[1,3,16,32,256]{4,2,3,1,0:T(8,128)}, f32[16,32,256]{2,0,1:T(8,128)}, f32[1,3,16,32,256]{4,2,3,1,0:T(8,128)}) fusion(f32[1,3,16,34,256]{4,2,3,1,0:T(8,128)S(1)} %get-tuple-element.57, f32[16,32,256]{2,0,1:T(8,128)} %get-tuple-element.112, f32[3]{0:T(128)S(1)} %compare_convert_fusion, ...), kind=kLoop, calls=%fused_computation.290 | loop fusion | flops 13107200 | bytes 23265796 | tf_op jit(solution)/shard_map/reduce_sum | solution.py:99
  528.7 7.2 %psum.216 = f32[]{:T(128)} all-reduce(f32[]{:T(128)} %get-tuple-element.19), channel_id=1, replica_groups=mesh['img_0'=4,'img_1'=4,'tile_0'=4,'tile_1'=2] {'img_0'}, use_global_device_ids=true, to_apply=%region_53.54 | all-reduce | flops 1 | bytes 8 | tf_op jit(solution)/shard_map/psum | solution.py:69
  550.0 8.5 %psum.219 = f32[]{:T(128)} all-reduce(f32[]{:T(128)} %psum.218), channel_id=1, replica_groups=mesh['img_0'=4,'img_1'=4,'tile_0'=4,'tile_1'=2] {'tile_1'}, use_global_device_ids=true, to_apply=%region_56.57 | all-reduce | flops 1 | bytes 8 | tf_op jit(solution)/shard_map/psum | solution.py:69
  573.6 7.7 %multiply_reduce_fusion.2 = (f32[16,32,256]{2,0,1:T(8,128)}, f32[1,3,16,32,256]{4,2,3,1,0:T(8,128)}, f32[16,32,256]{2,0,1:T(8,128)}, f32[1,3,16,32,256]{4,2,3,1,0:T(8,128)}) fusion(f32[1,3,16,34,256]{4,2,3,1,0:T(8,128)S(1)} %get-tuple-element.55, f32[16,32,256]{2,0,1:T(8,128)} %get-tuple-element.108, f32[3]{0:T(128)S(1)} %compare_convert_fusion, ...), kind=kLoop, calls=%fused_computation.284 | loop fusion | flops 13107200 | bytes 23265796 | tf_op jit(solution)/shard_map/reduce_sum | solution.py:99
  599.4 7.7 %psum.220 = f32[]{:T(128)} all-reduce(f32[]{:T(128)} %get-tuple-element.13), channel_id=1, replica_groups=mesh['img_0'=4,'img_1'=4,'tile_0'=4,'tile_1'=2] {'img_0'}, use_global_device_ids=true, to_apply=%region_62.63 | all-reduce | flops 1 | bytes 8 | tf_op jit(solution)/shard_map/psum | solution.py:69
  607.1 7.5 %psum.221 = f32[]{:T(128)} all-reduce(f32[]{:T(128)} %psum.220), channel_id=1, replica_groups=mesh['img_0'=4,'img_1'=4,'tile_0'=4,'tile_1'=2] {'img_1'}, use_global_device_ids=true, to_apply=%region_63.64 | all-reduce | flops 1 | bytes 8 | tf_op jit(solution)/shard_map/psum | solution.py:69
  614.6 7.1 %psum.222 = f32[]{:T(128)} all-reduce(f32[]{:T(128)} %psum.221), channel_id=1, replica_groups=mesh['img_0'=4,'img_1'=4,'tile_0'=4,'tile_1'=2] {'tile_0'}, use_global_device_ids=true, to_apply=%region_64.65 | all-reduce | flops 1 | bytes 8 | tf_op jit(solution)/shard_map/psum | solution.py:69
  621.8 8.5 %psum.223 = f32[]{:T(128)} all-reduce(f32[]{:T(128)} %psum.222), channel_id=1, replica_groups=mesh['img_0'=4,'img_1'=4,'tile_0'=4,'tile_1'=2] {'tile_1'}, use_global_device_ids=true, to_apply=%region_65.66 | all-reduce | flops 1 | bytes 8 | tf_op jit(solution)/shard_map/psum | solution.py:69
  (284 shorter events, 310.5 us)
Async XLA Ops:
  2.3 37.2 %collective-permute-start = (f32[1,3,16,32,256]{4,2,3,1,0:T(8,128)S(1)}, f32[1,3,16,32,256]{4,2,3,1,0:T(8,128)S(1)}, u32[]{:S(2)}, u32[]{:S(2)}) collective-permute-start(f32[1,3,16,32,256]{4,2,3,1,0:T(8,128)S(1)} %copy.34), channel_id=1, source_target_pairs={{0,8},{8,16},{16,24},{24,32},{32,40},{40,48},{48,56},{56,64},{64,7... | collective-permute-start | bytes 4718600 | tf_op jit(solution)/shard_map/ppermute | solution.py:27
  6.6 36.8 %collective-permute-start.1 = (f32[1,3,16,32,256]{4,2,3,1,0:T(8,128)S(1)}, f32[1,3,16,32,256]{4,2,3,1,0:T(8,128)S(1)}, u32[]{:S(2)}, u32[]{:S(2)}) collective-permute-start(f32[1,3,16,32,256]{4,2,3,1,0:T(8,128)S(1)} %copy.34), channel_id=1, source_target_pairs={{8,0},{16,8},{24,16},{32,24},{40,32},{48,40},{56,48},{64,56},{72,6... | collective-permute-start | bytes 4718600 | tf_op jit(solution)/shard_map/ppermute | solution.py:29
  46.7 7.2 %collective-permute-start.2 = (f32[3,3,16,1,256]{4,2,3,1,0:T(8,128)S(1)}, f32[3,3,16,1,256]{4,2,3,1,0:T(8,128)S(1)}, u32[]{:S(2)}, u32[]{:S(2)}) collective-permute-start(f32[3,3,16,1,256]{4,2,3,1,0:T(8,128)S(1)} %get-tuple-element.73), channel_id=1, source_target_pairs={{0,1},{1,2},{2,3},{3,4},{4,5},{5,6},{6,7},{8,9},{9,10},{10,11},{11... | collective-permute-start | bytes 442376 | tf_op jit(solution)/shard_map/ppermute | solution.py:27
  51.6 6.5 %collective-permute-start.3 = (f32[3,3,16,1,256]{4,2,3,1,0:T(8,128)S(1)}, f32[3,3,16,1,256]{4,2,3,1,0:T(8,128)S(1)}, u32[]{:S(2)}, u32[]{:S(2)}) collective-permute-start(f32[3,3,16,1,256]{4,2,3,1,0:T(8,128)S(1)} %get-tuple-element.74), channel_id=1, source_target_pairs={{1,0},{2,1},{3,2},{4,3},{5,4},{6,5},{7,6},{9,8},{10,9},{11,10},{12... | collective-permute-start | bytes 442376 | tf_op jit(solution)/shard_map/ppermute | solution.py:29
  82.7 15.4 %all-to-all-start = ((f32[16,1,1]{2,1,0:T(1,128)}), f32[16,1,1]{2,1,0:T(1,128)S(1)}, u32[]{:S(2)}, u32[]{:S(2)}) async-start(f32[16,1,1]{2,1,0:T(1,128)} %broadcast_in_dim.22), calls=%async_computation | async-start | bytes 16384 | tf_op jit(solution)/shard_map/all_to_all | solution.py:38
  98.8 9.6 %all-to-all-start.1 = ((f32[16,1,1]{2,1,0:T(1,128)}), f32[16,1,1]{2,1,0:T(1,128)S(1)}, u32[]{:S(2)}, u32[]{:S(2)}) async-start(f32[16,1,1]{2,1,0:T(1,128)} %broadcast_in_dim.24), calls=%async_computation.1 | async-start | bytes 16384 | tf_op jit(solution)/shard_map/all_to_all | solution.py:38
  122.3 12.1 %collective-permute-start.4 = (f32[1,3,16,1,256]{4,2,3,1,0:T(8,128)S(1)}, f32[1,3,16,1,256]{4,2,3,1,0:T(8,128)S(1)}, u32[]{:S(2)}, u32[]{:S(2)}) collective-permute-start(f32[1,3,16,1,256]{4,2,3,1,0:T(8,128)S(1)} %get-tuple-element.103), channel_id=1, source_target_pairs={{0,1},{1,2},{2,3},{3,4},{4,5},{5,6},{6,7},{8,9},{9,10},{10,11},{11... | collective-permute-start | bytes 147464 | tf_op jit(solution)/shard_map/ppermute | solution.py:27
  128.7 5.7 collective-permute-start.5
  182.5 4.3 collective-permute-start.6
  184.5 5.4 collective-permute-start.7
  205.8 4.4 collective-permute-start.8
  207.7 5.4 collective-permute-start.9
  253.7 4.3 collective-permute-start.10
  255.7 5.4 collective-permute-start.11
  277.0 4.4 collective-permute-start.12
  278.9 5.4 collective-permute-start.13
  324.8 37.5 %collective-permute-start.15 = (f32[1,3,16,32,256]{4,2,3,1,0:T(8,128)S(1)}, f32[1,3,16,32,256]{4,2,3,1,0:T(8,128)S(1)}, u32[]{:S(2)}, u32[]{:S(2)}) collective-permute-start(f32[1,3,16,32,256]{4,2,3,1,0:T(8,128)S(1)} %divide_subtract_fusion.4), channel_id=1, source_target_pairs={{8,0},{16,8},{24,16},{32,24},{40,32},{48,40},{56,48},{64,56},{72,6... | collective-permute-start | bytes 4718600 | tf_op jit(solution)/shard_map/ppermute | solution.py:29
  326.1 37.1 %collective-permute-start.14 = (f32[1,3,16,32,256]{4,2,3,1,0:T(8,128)S(1)}, f32[1,3,16,32,256]{4,2,3,1,0:T(8,128)S(1)}, u32[]{:S(2)}, u32[]{:S(2)}) collective-permute-start(f32[1,3,16,32,256]{4,2,3,1,0:T(8,128)S(1)} %divide_subtract_fusion.4), channel_id=1, source_target_pairs={{0,8},{8,16},{16,24},{24,32},{32,40},{40,48},{48,56},{56,64},{64,7... | collective-permute-start | bytes 4718600 | tf_op jit(solution)/shard_map/ppermute | solution.py:27
  363.2 5.2 collective-permute-start.16
  366.3 6.5 %collective-permute-start.17 = (f32[3,3,16,1,256]{4,2,3,1,0:T(8,128)S(1)}, f32[3,3,16,1,256]{4,2,3,1,0:T(8,128)S(1)}, u32[]{:S(2)}, u32[]{:S(2)}) collective-permute-start(f32[3,3,16,1,256]{4,2,3,1,0:T(8,128)S(1)} %get-tuple-element.72), channel_id=1, source_target_pairs={{1,0},{2,1},{3,2},{4,3},{5,4},{6,5},{7,6},{9,8},{10,9},{11,10},{12... | collective-permute-start | bytes 442376 | tf_op jit(solution)/shard_map/ppermute | solution.py:29
  394.6 13.3 %all-to-all-start.2 = ((f32[16,1,1]{2,1,0:T(1,128)}), f32[16,1,1]{2,1,0:T(1,128)S(1)}, u32[]{:S(2)}, u32[]{:S(2)}) async-start(f32[16,1,1]{2,1,0:T(1,128)} %broadcast_in_dim.27), calls=%async_computation.2 | async-start | bytes 16384 | tf_op jit(solution)/shard_map/all_to_all | solution.py:38
  408.5 9.8 %all-to-all-start.3 = ((f32[16,1,1]{2,1,0:T(1,128)}), f32[16,1,1]{2,1,0:T(1,128)S(1)}, u32[]{:S(2)}, u32[]{:S(2)}) async-start(f32[16,1,1]{2,1,0:T(1,128)} %broadcast_in_dim.29), calls=%async_computation.3 | async-start | bytes 16384 | tf_op jit(solution)/shard_map/all_to_all | solution.py:38
  432.0 12.3 %collective-permute-start.18 = (f32[1,3,16,1,256]{4,2,3,1,0:T(8,128)S(1)}, f32[1,3,16,1,256]{4,2,3,1,0:T(8,128)S(1)}, u32[]{:S(2)}, u32[]{:S(2)}) collective-permute-start(f32[1,3,16,1,256]{4,2,3,1,0:T(8,128)S(1)} %get-tuple-element.91), channel_id=1, source_target_pairs={{0,1},{1,2},{2,3},{3,4},{4,5},{5,6},{6,7},{8,9},{9,10},{10,11},{11... | collective-permute-start | bytes 147464 | tf_op jit(solution)/shard_map/ppermute | solution.py:27
  438.5 5.9 collective-permute-start.19
  490.6 4.3 collective-permute-start.20
  492.6 5.4 collective-permute-start.21
  513.9 4.6 collective-permute-start.22
  515.8 5.4 collective-permute-start.23
  561.5 4.3 collective-permute-start.24
  563.4 5.4 collective-permute-start.25
  584.6 4.4 collective-permute-start.26
  586.6 5.4 collective-permute-start.27
  (50 other events, 384.3 us)
where the time goes:
time: 644 us; the launch traced here: 635 us
  blocking collectives  208 us (32%)
  other arithmetic  169 us (26%)
  waiting for transfers between devices  121 us (19%)
  starting transfers between devices  98.1 us (15%)
  local copies, waits for them, and re-layouts  22.4 us (3%)
  between operations  16.4 us (3%)
    psum x24, blocking collectives, over_axes(): shard = lax.psum(shard, axis)  186 us
    ppermute x14, waiting for transfers between devices, padded_2(): lax.ppermute(head, axis, [((i + 1) % count, i) for i in range(ends)])  65.9 us
    reduce_sum x6, other arithmetic, hessian_point(): projected = jnp.sum(middle * vector, axis=-4, keepdims=True)  47.5 us
    ppermute x14, starting transfers between devices, padded_2(): lax.ppermute(tail, axis, [(i, (i + 1) % count) for i in range(ends)])  44.6 us
    reduce_sum x6, other arithmetic, body(): grad_total = over_axes(jnp.sum(gradients * gradients), IMG_TILE)  33.5 us
    ppermute x14, waiting for transfers between devices, padded_2(): lax.ppermute(tail, axis, [(i, (i + 1) % count) for i in range(ends)])  32.7 us
    ppermute x14, starting transfers between devices, padded_2(): lax.ppermute(head, axis, [((i + 1) % count, i) for i in range(ends)])  30.5 us
    all_to_all x4, starting transfers between devices, from_everyone(): lax.all_to_all(jnp.broadcast_to(shard[None], (peers, *shard.shape)), axis...  23 us
  transfers between devices with their start and end apart: 32, of which 19 were waited for; matrix products, arithmetic and copies ran while one was open for 1% of the time, Pallas kernels for 0%

commit v1 on v0

--- a/solution.py
+++ b/solution.py
@@ -66,7 +66,8 @@
 
 def over_axes(shard, axes):
     for axis in axes:
-        shard = lax.psum(shard, axis)
+        parts = lax.all_gather(shard, axis, axis=0, tiled=False)
+        shard = parts.sum(axis=0)
     return shard
 
 

time: 644 us -> 671 us (1.042)
  local copies, waits for them, and re-layouts: 22.4 us -> 54.4 us
  other arithmetic: 169 us -> 185 us
  blocking collectives: 208 us -> 192 us
    psum x24 -> x0, blocking collectives: 186 us -> none  [over_axes(): shard = lax.psum(shard, axis)]
    unnamed x0 -> x24, blocking collectives: none -> 170 us
    unnamed x104 -> x168, local copies, waits for them, and re-layouts: 15.3 us -> 47.3 us
    ppermute x14, waiting for transfers between devices: 32.7 us -> 63.8 us  [padded_2(): lax.ppermute(tail, axis, [(i, (i + 1) % count) for i in range(ends)])]
    ppermute x14, waiting for transfers between devices: 65.9 us -> 36.3 us  [padded_2(): lax.ppermute(head, axis, [((i + 1) % count, i) for i in range(ends)])]
    reduce_sum x0 -> x24, other arithmetic: none -> 14.7 us  [over_axes(): shard = parts.sum(axis=0)]
  transfers between devices with their start and end apart: 32 -> 32, of which waited for: 19 -> 19; matrix products, arithmetic and copies ran while one was open for 1% -> 2% of each run, Pallas kernels for 0% -> 0%
where the time goes in v1:
time: 671 us; the launch traced here: 661 us
  blocking collectives  192 us (29%)
  other arithmetic  185 us (28%)
  waiting for transfers between devices  116 us (17%)
  starting transfers between devices  97.2 us (14%)
  local copies, waits for them, and re-layouts  54.4 us (8%)
  between operations  16.5 us (2%)
    unnamed x24, blocking collectives  170 us
    ppermute x14, waiting for transfers between devices, padded_2(): lax.ppermute(tail, axis, [(i, (i + 1) % count) for i in range(ends)])  63.8 us
    reduce_sum x6, other arithmetic, hessian_point(): projected = jnp.sum(middle * vector, axis=-4, keepdims=True)  47.7 us
    unnamed x168, local copies, waits for them, and re-layouts  47.3 us
    ppermute x14, starting transfers between devices, padded_2(): lax.ppermute(tail, axis, [(i, (i + 1) % count) for i in range(ends)])  42.9 us
    ppermute x14, waiting for transfers between devices, padded_2(): lax.ppermute(head, axis, [((i + 1) % count, i) for i in range(ends)])  36.3 us
    reduce_sum x6, other arithmetic, body(): grad_total = over_axes(jnp.sum(gradients * gradients), IMG_TILE)  33.4 us
    ppermute x14, starting transfers between devices, padded_2(): lax.ppermute(head, axis, [((i + 1) % count, i) for i in range(ends)])  31 us
  transfers between devices with their start and end apart: 32, of which 19 were waited for; matrix products, arithmetic and copies ran while one was open for 2% of the time, Pallas kernels for 0%

profile of v1, /device:TPU:1, one launch (start us, length us, event | category | flops | bytes accessed | tf_op | source)
XLA Modules:
  0.0 661.3 jit_solution(2426854586880087857)
XLA Ops:
  7.9 31.6 %collective-permute-done = f32[1,3,16,32,256]{4,2,3,1,0:T(8,128)S(1)} collective-permute-done((f32[1,3,16,32,256]{4,2,3,1,0:T(8,128)S(1)}, f32[1,3,16,32,256]{4,2,3,1,0:T(8,128)S(1)}, u32[]{:S(2)}, u32[]{:S(2)}) %collective-permute-start) | collective-permute-done | bytes 1572896 | tf_op jit(solution)/shard_map/ppermute | solution.py:27
  65.9 11.1 %all-reduce.43 = (f32[1]{0:T(128)}, f32[1]{0:T(128)}) all-reduce(f32[1]{0:T(128)} %bitcast.1, f32[1]{0:T(128)} %bitcast.3), channel_id=1, replica_groups=mesh['img_0'=4,'img_1'=4,'tile_0'=4,'tile_1'=2] {'tile_0','tile_1'}, use_global_device_ids=true, to_apply=%region_1.2 | all-reduce | flops 2 | bytes 16 | tf_op jit(solution)/shard_map/psum | solution.py:138
  78.3 9.1 %all-to-all-start = ((f32[16,1,1]{2,1,0:T(1,128)}), f32[16,1,1]{2,1,0:T(1,128)S(1)}, u32[]{:S(2)}, u32[]{:S(2)}) async-start(f32[16,1,1]{2,1,0:T(1,128)} %broadcast_in_dim.22), calls=%async_computation | async-start | bytes 16384 | tf_op jit(solution)/shard_map/all_to_all | solution.py:38
  106.3 8.5 %multiply_reduce_fusion.28 = (f32[16,32,256]{2,0,1:T(8,128)S(1)}, f32[1,3,16,32,256]{4,2,3,1,0:T(8,128)S(1)}, f32[16,32,256]{2,0,1:T(8,128)S(1)}, f32[1,3,16,32,256]{4,2,3,1,0:T(8,128)S(1)}) fusion(f32[1,3,16,34,256]{4,2,3,1,0:T(8,128)} %get-tuple-element.67, f32[16,32,256]{2,0,1:T(8,128)S(1)} %get-tuple-element.128, f32[3]{0:T(128)S(1)} %compare_convert_fusion, ...), kind=kLoop, calls=%fused_computation.318 | loop fusion | flops 8388608 | bytes 19496976 | tf_op jit(solution)/shard_map/reduce_sum | solution.py:100
  135.2 7.2 %multiply_reduce_fusion.26 = (f32[]{:T(128)}, f32[1,3,16,32,256]{4,2,3,1,0:T(8,128)}, f32[1,3,16,32,256]{4,2,3,1,0:T(8,128)}) fusion(f32[]{:T(128)} %bitcast.10, f32[16,32,256]{2,0,1:T(8,128)} %broadcast_multiply_fusion.10, f32[1,3,16,34,256]{4,2,3,1,0:T(8,128)S(1)} %get-tuple-element.68, f32[1,3,16,32,256]{4,2,3,1,0:T(8,128)} %copy-done.39, ...), kind=kLoop, calls=%fused_computation.315 | loop fusion | flops 13369343 | bytes 23167004 | tf_op jit(solution)/shard_map/reduce_sum | solution.py:185
  144.4 6.8 %all-reduce.18 = f32[4]{0:T(128)S(1)} all-reduce(f32[4]{0:T(128)S(1)} %dynamic-update-slice), channel_id=1, replica_groups=mesh['img_0'=4,'img_1'=4,'tile_0'=4,'tile_1'=2] {'img_0'}, use_global_device_ids=true, to_apply=%add.18 | all-reduce | flops 4 | bytes 32
  153.7 7.0 %all-reduce.19 = f32[4]{0:T(128)S(1)} all-reduce(f32[4]{0:T(128)S(1)} %dynamic-update-slice.1), channel_id=1, replica_groups=mesh['img_0'=4,'img_1'=4,'tile_0'=4,'tile_1'=2] {'img_1'}, use_global_device_ids=true, to_apply=%add.19 | all-reduce | flops 4 | bytes 32
  163.4 6.6 %all-reduce.20 = f32[4]{0:T(128)S(1)} all-reduce(f32[4]{0:T(128)S(1)} %dynamic-update-slice.2), channel_id=1, replica_groups=mesh['img_0'=4,'img_1'=4,'tile_0'=4,'tile_1'=2] {'tile_0'}, use_global_device_ids=true, to_apply=%add.20 | all-reduce | flops 4 | bytes 32
  172.0 9.9 %all-reduce.21 = f32[2]{0:T(128)S(1)} all-reduce(f32[2]{0:T(128)S(1)} %dynamic-update-slice.3), channel_id=1, replica_groups=mesh['img_0'=4,'img_1'=4,'tile_0'=4,'tile_1'=2] {'tile_1'}, use_global_device_ids=true, to_apply=%add.21 | all-reduce | flops 2 | bytes 16
  198.7 7.8 %multiply_reduce_fusion.23 = (f32[16,32,256]{2,0,1:T(8,128)}, f32[1,3,16,32,256]{4,2,3,1,0:T(8,128)}, f32[16,32,256]{2,0,1:T(8,128)}, f32[1,3,16,32,256]{4,2,3,1,0:T(8,128)}) fusion(f32[1,3,16,34,256]{4,2,3,1,0:T(8,128)S(1)} %get-tuple-element.61, f32[16,32,256]{2,0,1:T(8,128)} %get-tuple-element.124, f32[3]{0:T(128)S(1)} %compare_convert_fusion, ...), kind=kLoop, calls=%fused_computation.311 | loop fusion | flops 13107200 | bytes 23265796 | tf_op jit(solution)/shard_map/reduce_sum | solution.py:100
  233.3 6.7 %all-reduce.23 = f32[4]{0:T(128)S(1)} all-reduce(f32[4]{0:T(128)S(1)} %dynamic-update-slice.5), channel_id=1, replica_groups=mesh['img_0'=4,'img_1'=4,'tile_0'=4,'tile_1'=2] {'img_1'}, use_global_device_ids=true, to_apply=%add.23 | all-reduce | flops 4 | bytes 32
  241.9 6.4 all-reduce.24
  250.4 7.8 %all-reduce.25 = f32[2]{0:T(128)S(1)} all-reduce(f32[2]{0:T(128)S(1)} %dynamic-update-slice.7), channel_id=1, replica_groups=mesh['img_0'=4,'img_1'=4,'tile_0'=4,'tile_1'=2] {'tile_1'}, use_global_device_ids=true, to_apply=%add.25 | all-reduce | flops 2 | bytes 16
  273.9 7.7 %multiply_reduce_fusion.18 = (f32[16,32,256]{2,0,1:T(8,128)}, f32[1,3,16,32,256]{4,2,3,1,0:T(8,128)}, f32[16,32,256]{2,0,1:T(8,128)}, f32[1,3,16,32,256]{4,2,3,1,0:T(8,128)}) fusion(f32[1,3,16,34,256]{4,2,3,1,0:T(8,128)S(1)} %get-tuple-element.59, f32[16,32,256]{2,0,1:T(8,128)} %get-tuple-element.120, f32[3]{0:T(128)S(1)} %compare_convert_fusion, ...), kind=kLoop, calls=%fused_computation.305 | loop fusion | flops 13107200 | bytes 23265796 | tf_op jit(solution)/shard_map/reduce_sum | solution.py:100
  300.1 6.7 %all-reduce.26 = f32[4]{0:T(128)S(1)} all-reduce(f32[4]{0:T(128)S(1)} %dynamic-update-slice.8), channel_id=1, replica_groups=mesh['img_0'=4,'img_1'=4,'tile_0'=4,'tile_1'=2] {'img_0'}, use_global_device_ids=true, to_apply=%add.26 | all-reduce | flops 4 | bytes 32
  308.6 7.0 %all-reduce.27 = f32[4]{0:T(128)S(1)} all-reduce(f32[4]{0:T(128)S(1)} %dynamic-update-slice.9), channel_id=1, replica_groups=mesh['img_0'=4,'img_1'=4,'tile_0'=4,'tile_1'=2] {'img_1'}, use_global_device_ids=true, to_apply=%add.27 | all-reduce | flops 4 | bytes 32
  326.1 7.9 %all-reduce.29 = f32[2]{0:T(128)S(1)} all-reduce(f32[2]{0:T(128)S(1)} %dynamic-update-slice.11), channel_id=1, replica_groups=mesh['img_0'=4,'img_1'=4,'tile_0'=4,'tile_1'=2] {'tile_1'}, use_global_device_ids=true, to_apply=%add.29 | all-reduce | flops 2 | bytes 16
  340.7 32.0 %collective-permute-done.14 = f32[1,3,16,32,256]{4,2,3,1,0:T(8,128)S(1)} collective-permute-done((f32[1,3,16,32,256]{4,2,3,1,0:T(8,128)S(1)}, f32[1,3,16,32,256]{4,2,3,1,0:T(8,128)S(1)}, u32[]{:S(2)}, u32[]{:S(2)}) %collective-permute-start.14) | collective-permute-done | bytes 1572896 | tf_op jit(solution)/shard_map/ppermute | solution.py:27
  394.1 10.1 %all-reduce.42 = (f32[1]{0:T(128)}, f32[1]{0:T(128)}) all-reduce(f32[1]{0:T(128)} %bitcast.27, f32[1]{0:T(128)} %bitcast.29), channel_id=1, replica_groups=mesh['img_0'=4,'img_1'=4,'tile_0'=4,'tile_1'=2] {'tile_0','tile_1'}, use_global_device_ids=true, to_apply=%region_34.35 | all-reduce | flops 2 | bytes 16 | tf_op jit(solution)/shard_map/psum | solution.py:138
  405.5 6.7 %all-to-all-start.2 = ((f32[16,1,1]{2,1,0:T(1,128)}), f32[16,1,1]{2,1,0:T(1,128)S(1)}, u32[]{:S(2)}, u32[]{:S(2)}) async-start(f32[16,1,1]{2,1,0:T(1,128)} %broadcast_in_dim.27), calls=%async_computation.2 | async-start | bytes 16384 | tf_op jit(solution)/shard_map/all_to_all | solution.py:38
  431.2 8.2 %multiply_reduce_fusion.12 = (f32[16,32,256]{2,0,1:T(8,128)S(1)}, f32[1,3,16,32,256]{4,2,3,1,0:T(8,128)S(1)}, f32[16,32,256]{2,0,1:T(8,128)S(1)}, f32[1,3,16,32,256]{4,2,3,1,0:T(8,128)S(1)}) fusion(f32[1,3,16,34,256]{4,2,3,1,0:T(8,128)} %get-tuple-element.63, f32[16,32,256]{2,0,1:T(8,128)S(1)} %get-tuple-element.116, f32[3]{0:T(128)S(1)} %compare_convert_fusion, ...), kind=kLoop, calls=%fused_computation.297 | loop fusion | flops 8388608 | bytes 19496976 | tf_op jit(solution)/shard_map/reduce_sum | solution.py:100
  460.2 7.3 %multiply_reduce_fusion.10 = (f32[]{:T(128)}, f32[1,3,16,32,256]{4,2,3,1,0:T(8,128)}, f32[1,3,16,32,256]{4,2,3,1,0:T(8,128)}) fusion(f32[]{:T(128)} %bitcast.10, f32[16,32,256]{2,0,1:T(8,128)} %broadcast_multiply_fusion.4, f32[1,3,16,34,256]{4,2,3,1,0:T(8,128)S(1)} %get-tuple-element.64, f32[1,3,16,32,256]{4,2,3,1,0:T(8,128)} %copy-done.37, ...), kind=kLoop, calls=%fused_computation.294 | loop fusion | flops 13369343 | bytes 23167004 | tf_op jit(solution)/shard_map/reduce_sum | solution.py:185
  468.8 7.1 %all-reduce.30 = f32[4]{0:T(128)S(1)} all-reduce(f32[4]{0:T(128)S(1)} %dynamic-update-slice.12), channel_id=1, replica_groups=mesh['img_0'=4,'img_1'=4,'tile_0'=4,'tile_1'=2] {'img_0'}, use_global_device_ids=true, to_apply=%add.30 | all-reduce | flops 4 | bytes 32
  477.8 7.0 %all-reduce.31 = f32[4]{0:T(128)S(1)} all-reduce(f32[4]{0:T(128)S(1)} %dynamic-update-slice.13), channel_id=1, replica_groups=mesh['img_0'=4,'img_1'=4,'tile_0'=4,'tile_1'=2] {'img_1'}, use_global_device_ids=true, to_apply=%add.31 | all-reduce | flops 4 | bytes 32
  494.7 9.4 %all-reduce.33 = f32[2]{0:T(128)S(1)} all-reduce(f32[2]{0:T(128)S(1)} %dynamic-update-slice.15), channel_id=1, replica_groups=mesh['img_0'=4,'img_1'=4,'tile_0'=4,'tile_1'=2] {'tile_1'}, use_global_device_ids=true, to_apply=%add.33 | all-reduce | flops 2 | bytes 16
  520.3 7.8 %multiply_reduce_fusion.7 = (f32[16,32,256]{2,0,1:T(8,128)}, f32[1,3,16,32,256]{4,2,3,1,0:T(8,128)}, f32[16,32,256]{2,0,1:T(8,128)}, f32[1,3,16,32,256]{4,2,3,1,0:T(8,128)}) fusion(f32[1,3,16,34,256]{4,2,3,1,0:T(8,128)S(1)} %get-tuple-element.57, f32[16,32,256]{2,0,1:T(8,128)} %get-tuple-element.112, f32[3]{0:T(128)S(1)} %compare_convert_fusion, ...), kind=kLoop, calls=%fused_computation.290 | loop fusion | flops 13107200 | bytes 23265796 | tf_op jit(solution)/shard_map/reduce_sum | solution.py:100
  546.6 6.6 all-reduce.34
  571.8 7.8 %all-reduce.37 = f32[2]{0:T(128)S(1)} all-reduce(f32[2]{0:T(128)S(1)} %dynamic-update-slice.19), channel_id=1, replica_groups=mesh['img_0'=4,'img_1'=4,'tile_0'=4,'tile_1'=2] {'tile_1'}, use_global_device_ids=true, to_apply=%add.37 | all-reduce | flops 2 | bytes 16
  595.3 7.7 %multiply_reduce_fusion.2 = (f32[16,32,256]{2,0,1:T(8,128)}, f32[1,3,16,32,256]{4,2,3,1,0:T(8,128)}, f32[16,32,256]{2,0,1:T(8,128)}, f32[1,3,16,32,256]{4,2,3,1,0:T(8,128)}) fusion(f32[1,3,16,34,256]{4,2,3,1,0:T(8,128)S(1)} %get-tuple-element.55, f32[16,32,256]{2,0,1:T(8,128)} %get-tuple-element.108, f32[3]{0:T(128)S(1)} %compare_convert_fusion, ...), kind=kLoop, calls=%fused_computation.284 | loop fusion | flops 13107200 | bytes 23265796 | tf_op jit(solution)/shard_map/reduce_sum | solution.py:100
  621.6 7.0 %all-reduce.38 = f32[4]{0:T(128)S(1)} all-reduce(f32[4]{0:T(128)S(1)} %dynamic-update-slice.20), channel_id=1, replica_groups=mesh['img_0'=4,'img_1'=4,'tile_0'=4,'tile_1'=2] {'img_0'}, use_global_device_ids=true, to_apply=%add.38 | all-reduce | flops 4 | bytes 32
  630.5 6.8 %all-reduce.39 = f32[4]{0:T(128)S(1)} all-reduce(f32[4]{0:T(128)S(1)} %dynamic-update-slice.21), channel_id=1, replica_groups=mesh['img_0'=4,'img_1'=4,'tile_0'=4,'tile_1'=2] {'img_1'}, use_global_device_ids=true, to_apply=%add.39 | all-reduce | flops 4 | bytes 32
  647.9 7.8 %all-reduce.41 = f32[2]{0:T(128)S(1)} all-reduce(f32[2]{0:T(128)S(1)} %dynamic-update-slice.23), channel_id=1, replica_groups=mesh['img_0'=4,'img_1'=4,'tile_0'=4,'tile_1'=2] {'tile_1'}, use_global_device_ids=true, to_apply=%add.41 | all-reduce | flops 2 | bytes 16
  (372 shorter events, 349.5 us)
Async XLA Ops:
  2.3 37.2 %collective-permute-start = (f32[1,3,16,32,256]{4,2,3,1,0:T(8,128)S(1)}, f32[1,3,16,32,256]{4,2,3,1,0:T(8,128)S(1)}, u32[]{:S(2)}, u32[]{:S(2)}) collective-permute-start(f32[1,3,16,32,256]{4,2,3,1,0:T(8,128)S(1)} %copy.34), channel_id=1, source_target_pairs={{0,8},{8,16},{16,24},{24,32},{32,40},{40,48},{48,56},{56,64},{64,7... | collective-permute-start | bytes 4718600 | tf_op jit(solution)/shard_map/ppermute | solution.py:27
  6.6 36.8 %collective-permute-start.1 = (f32[1,3,16,32,256]{4,2,3,1,0:T(8,128)S(1)}, f32[1,3,16,32,256]{4,2,3,1,0:T(8,128)S(1)}, u32[]{:S(2)}, u32[]{:S(2)}) collective-permute-start(f32[1,3,16,32,256]{4,2,3,1,0:T(8,128)S(1)} %copy.34), channel_id=1, source_target_pairs={{8,0},{16,8},{24,16},{32,24},{40,32},{48,40},{56,48},{64,56},{72,6... | collective-permute-start | bytes 4718600 | tf_op jit(solution)/shard_map/ppermute | solution.py:29
  44.6 7.8 %collective-permute-start.2 = (f32[3,3,16,1,256]{4,2,3,1,0:T(8,128)S(1)}, f32[3,3,16,1,256]{4,2,3,1,0:T(8,128)S(1)}, u32[]{:S(2)}, u32[]{:S(2)}) collective-permute-start(f32[3,3,16,1,256]{4,2,3,1,0:T(8,128)S(1)} %get-tuple-element.73), channel_id=1, source_target_pairs={{0,1},{1,2},{2,3},{3,4},{4,5},{5,6},{6,7},{8,9},{9,10},{10,11},{11... | collective-permute-start | bytes 442376 | tf_op jit(solution)/shard_map/ppermute | solution.py:27
  49.5 6.5 collective-permute-start.3
  78.3 15.4 %all-to-all-start = ((f32[16,1,1]{2,1,0:T(1,128)}), f32[16,1,1]{2,1,0:T(1,128)S(1)}, u32[]{:S(2)}, u32[]{:S(2)}) async-start(f32[16,1,1]{2,1,0:T(1,128)} %broadcast_in_dim.22), calls=%async_computation | async-start | bytes 16384 | tf_op jit(solution)/shard_map/all_to_all | solution.py:38
  94.3 10.0 %all-to-all-start.1 = ((f32[16,1,1]{2,1,0:T(1,128)}), f32[16,1,1]{2,1,0:T(1,128)S(1)}, u32[]{:S(2)}, u32[]{:S(2)}) async-start(f32[16,1,1]{2,1,0:T(1,128)} %broadcast_in_dim.24), calls=%async_computation.1 | async-start | bytes 16384 | tf_op jit(solution)/shard_map/all_to_all | solution.py:38
  117.6 13.4 %collective-permute-start.4 = (f32[1,3,16,1,256]{4,2,3,1,0:T(8,128)S(1)}, f32[1,3,16,1,256]{4,2,3,1,0:T(8,128)S(1)}, u32[]{:S(2)}, u32[]{:S(2)}) collective-permute-start(f32[1,3,16,1,256]{4,2,3,1,0:T(8,128)S(1)} %get-tuple-element.103), channel_id=1, source_target_pairs={{0,1},{1,2},{2,3},{3,4},{4,5},{5,6},{6,7},{8,9},{9,10},{10,11},{11... | collective-permute-start | bytes 147464 | tf_op jit(solution)/shard_map/ppermute | solution.py:27
  123.6 7.5 %collective-permute-start.5 = (f32[1,3,16,1,256]{4,2,3,1,0:T(8,128)S(1)}, f32[1,3,16,1,256]{4,2,3,1,0:T(8,128)S(1)}, u32[]{:S(2)}, u32[]{:S(2)}) collective-permute-start(f32[1,3,16,1,256]{4,2,3,1,0:T(8,128)S(1)} %get-tuple-element.104), channel_id=1, source_target_pairs={{1,0},{2,1},{3,2},{4,3},{5,4},{6,5},{7,6},{9,8},{10,9},{11,10},{12... | collective-permute-start | bytes 147464 | tf_op jit(solution)/shard_map/ppermute | solution.py:29
  186.1 4.3 collective-permute-start.6
  188.0 5.4 collective-permute-start.7
  208.8 5.0 collective-permute-start.8
  210.8 5.4 collective-permute-start.9
  261.7 4.3 collective-permute-start.10
  263.7 5.4 collective-permute-start.11
  283.9 4.6 collective-permute-start.12
  286.0 5.4 collective-permute-start.13
  337.0 35.7 %collective-permute-start.14 = (f32[1,3,16,32,256]{4,2,3,1,0:T(8,128)S(1)}, f32[1,3,16,32,256]{4,2,3,1,0:T(8,128)S(1)}, u32[]{:S(2)}, u32[]{:S(2)}) collective-permute-start(f32[1,3,16,32,256]{4,2,3,1,0:T(8,128)S(1)} %divide_subtract_fusion.4), channel_id=1, source_target_pairs={{0,8},{8,16},{16,24},{24,32},{32,40},{40,48},{48,56},{56,64},{64,7... | collective-permute-start | bytes 4718600 | tf_op jit(solution)/shard_map/ppermute | solution.py:27
  339.4 37.2 %collective-permute-start.15 = (f32[1,3,16,32,256]{4,2,3,1,0:T(8,128)S(1)}, f32[1,3,16,32,256]{4,2,3,1,0:T(8,128)S(1)}, u32[]{:S(2)}, u32[]{:S(2)}) collective-permute-start(f32[1,3,16,32,256]{4,2,3,1,0:T(8,128)S(1)} %divide_subtract_fusion.4), channel_id=1, source_target_pairs={{8,0},{16,8},{24,16},{32,24},{40,32},{48,40},{56,48},{64,56},{72,6... | collective-permute-start | bytes 4718600 | tf_op jit(solution)/shard_map/ppermute | solution.py:29
  376.7 5.2 collective-permute-start.16
  379.8 6.5 collective-permute-start.17
  405.5 13.1 %all-to-all-start.2 = ((f32[16,1,1]{2,1,0:T(1,128)}), f32[16,1,1]{2,1,0:T(1,128)S(1)}, u32[]{:S(2)}, u32[]{:S(2)}) async-start(f32[16,1,1]{2,1,0:T(1,128)} %broadcast_in_dim.27), calls=%async_computation.2 | async-start | bytes 16384 | tf_op jit(solution)/shard_map/all_to_all | solution.py:38
  419.3 10.0 %all-to-all-start.3 = ((f32[16,1,1]{2,1,0:T(1,128)}), f32[16,1,1]{2,1,0:T(1,128)S(1)}, u32[]{:S(2)}, u32[]{:S(2)}) async-start(f32[16,1,1]{2,1,0:T(1,128)} %broadcast_in_dim.29), calls=%async_computation.3 | async-start | bytes 16384 | tf_op jit(solution)/shard_map/all_to_all | solution.py:38
  442.2 13.9 %collective-permute-start.18 = (f32[1,3,16,1,256]{4,2,3,1,0:T(8,128)S(1)}, f32[1,3,16,1,256]{4,2,3,1,0:T(8,128)S(1)}, u32[]{:S(2)}, u32[]{:S(2)}) collective-permute-start(f32[1,3,16,1,256]{4,2,3,1,0:T(8,128)S(1)} %get-tuple-element.91), channel_id=1, source_target_pairs={{0,1},{1,2},{2,3},{3,4},{4,5},{5,6},{6,7},{8,9},{9,10},{10,11},{11... | collective-permute-start | bytes 147464 | tf_op jit(solution)/shard_map/ppermute | solution.py:27
  448.5 7.5 %collective-permute-start.19 = (f32[1,3,16,1,256]{4,2,3,1,0:T(8,128)S(1)}, f32[1,3,16,1,256]{4,2,3,1,0:T(8,128)S(1)}, u32[]{:S(2)}, u32[]{:S(2)}) collective-permute-start(f32[1,3,16,1,256]{4,2,3,1,0:T(8,128)S(1)} %get-tuple-element.92), channel_id=1, source_target_pairs={{1,0},{2,1},{3,2},{4,3},{5,4},{6,5},{7,6},{9,8},{10,9},{11,10},{12... | collective-permute-start | bytes 147464 | tf_op jit(solution)/shard_map/ppermute | solution.py:29
  507.7 4.3 collective-permute-start.20
  509.6 5.4 collective-permute-start.21
  530.4 4.6 collective-permute-start.22
  532.5 5.4 collective-permute-start.23
  583.2 4.6 collective-permute-start.24
  585.1 5.4 collective-permute-start.25
  605.4 4.6 collective-permute-start.26
  607.4 5.4 collective-permute-start.27
  (56 other events, 474.9 us)
